TPU v7x, 512 devices: a whole 4x4x16 slice. The times are simulated.
512 devices in a mesh: layer: 4 (over y), prow: 16 (over z), pcol: 8 (over x, core).
Axes of the slice: x: 4, y: 4, z: 16, core: 2. Of those that a mesh axis runs over, the one named last changes fastest.
Arguments:
- own_blocks: bfloat16 [4, 21, 16, 128, 2, 8, 128], P('layer', None, 'prow', None, None, 'pcol'), may hold values from -0.046875 to 0.046875
- own_pattern: int32 [4, 21, 16, 2, 8], P('layer', None, 'prow', None, 'pcol'), may hold values 0 or 1
- own_inverse: bfloat16 [4, 3, 16, 128, 2, 8, 128], P('layer', None, 'prow', None, None, 'pcol'), as said below
- pair_blocks: bfloat16 [4, 12, 16, 128, 2, 8, 128], P('layer', None, 'prow', None, None, 'pcol'), as said below
- pair_inverse: bfloat16 [4, 3, 16, 128, 2, 8, 128], P('layer', None, 'prow', None, None, 'pcol'), as said below
- root_blocks: bfloat16 [3, 16, 128, 2, 8, 128], P(None, 'prow', None, None, 'pcol'), may hold values from -0.046875 to 0.046875
- root_inverse: bfloat16 [3, 16, 128, 2, 8, 128], P(None, 'prow', None, None, 'pcol'), as said below
- own_rhs: bfloat16 [4, 3, 16, 128, 256], P('layer', None, 'prow'), may hold values from -6 to 6
- shared_rhs: bfloat16 [4, 6, 16, 128, 256], P('layer', None, 'prow'), may hold values from -3 to 3
Outputs:
- own_solution: bfloat16 [4, 3, 2, 8, 128, 256], P('layer', None, None, 'pcol')
- pair_solution: bfloat16 [4, 3, 2, 8, 128, 256], P('layer', None, None, 'pcol')
- root_solution: bfloat16 [4, 3, 2, 8, 128, 256], P('layer', None, None, 'pcol')
Inputs may be any that keep to these rules, and one draw needn't show every extreme that they name: `pair_blocks`: layers 2m and 2m+1 hold equal copies of their parent's blocks. `pair_inverse`: each panel's inverse is lower triangular; layers 2m and 2m+1 hold equal copies. `own_inverse`: each panel's inverse is lower triangular. `root_inverse`: each panel's inverse is lower triangular.
All inputs are finite; a program needn't handle non-finite values. No bound on the sum of `own_pattern` on one device may be relied on, other than what follows from the above.
Results may differ from a plain program's by a relative error of at most 0.038.
Values may be sent and summed in bfloat16 or wider, within the bound.
No kernel may reach another device: no remote copies, remote signals or barrier semaphores. Data moves between devices by JAX's collectives and lax.ppermute only.
A program may use at most 64 MiB of HBM per device.

v0:
```python
import jax
import jax.numpy as jnp
from jax import lax
from jax.sharding import PartitionSpec as P


def from_partner(array, axis, apart):
    return lax.ppermute(array, axis, [(i, i ^ 1 << apart) for i in range(lax.axis_size(axis))])


def column_product(stacked, solved):
    block_count, row_count, col_width = stacked.shape
    flattened = stacked.reshape(block_count * row_count, col_width)
    product = jnp.dot(flattened, solved, preferred_element_type=jnp.float32)
    return product.reshape(block_count, row_count, solved.shape[1])


def row_total(partial_value):
    return lax.psum(partial_value.astype(jnp.bfloat16), "pcol").astype(jnp.float32)


def panel_solve(residual, inverse):
    rounded = residual.astype(jnp.bfloat16)
    partial_value = lax.dot_general(
        inverse, rounded, (((0,), (0,)), ((), ())), preferred_element_type=jnp.float32
    )
    return lax.psum(partial_value.astype(jnp.bfloat16), "prow")


def forward_solve(
    own_cols, own_inv, pair_cols, pair_inv, root_cols, root_inv, own_rows, shared_rows
):
    panels = own_inv.shape[0]
    chain_length = 3 * panels
    first_col = lax.axis_index("pcol") == 0
    solved = []
    updates_sum = jnp.zeros((chain_length,) + own_rows.shape[1:], jnp.float32)
    offset = 0
    for step_index in range(panels):
        residual = own_rows[step_index].astype(jnp.float32)
        if step_index > 0:
            residual = residual + row_total(-updates_sum[step_index])
        panel_result = panel_solve(residual, own_inv[step_index])
        solved.append(panel_result)
        block_count = chain_length - 1 - step_index
        update = column_product(own_cols[offset : offset + block_count], panel_result)
        updates_sum = updates_sum.at[step_index + 1 :].add(update)
        offset += block_count
    ancestors = jnp.where(first_col, shared_rows.astype(jnp.float32), 0.0) - updates_sum[panels:]
    ancestors = ancestors + from_partner(ancestors.astype(jnp.bfloat16), "layer", 0).astype(
        ancestors.dtype
    )
    parent_part = ancestors[:panels]
    inner_sums = jnp.zeros_like(ancestors)
    offset = 0
    for step_index in range(panels):
        residual = row_total(parent_part[step_index] - inner_sums[step_index])
        panel_result = panel_solve(residual, pair_inv[step_index])
        solved.append(panel_result)
        block_count = 2 * panels - 1 - step_index
        update = column_product(pair_cols[offset : offset + block_count], panel_result)
        inner_sums = inner_sums.at[step_index + 1 :].add(update)
        offset += block_count
    joined = ancestors[panels:] - inner_sums[panels:]
    joined = joined + from_partner(joined.astype(jnp.bfloat16), "layer", 1).astype(joined.dtype)
    root_sums = jnp.zeros_like(joined)
    offset = 0
    for step_index in range(panels):
        residual = row_total(joined[step_index] - root_sums[step_index])
        panel_result = panel_solve(residual, root_inv[step_index])
        solved.append(panel_result)
        block_count = panels - 1 - step_index
        if block_count > 0:
            update = column_product(root_cols[offset : offset + block_count], panel_result)
            root_sums = root_sums.at[step_index + 1 :].add(update)
            offset += block_count
    return solved


def local(
    own_blocks,
    own_pattern,
    own_inverse,
    pair_blocks,
    pair_inverse,
    root_blocks,
    root_inverse,
    own_rhs,
    shared_rhs,
):
    tile_rows = own_blocks.shape[3]
    cycles = own_blocks.shape[4]
    col_width = cycles * tile_rows
    rhs_width = own_rhs.shape[-1]
    own_tiles = own_blocks.reshape(-1, tile_rows, cycles, tile_rows)
    kept_tiles = own_pattern.reshape(-1, 1, cycles, 1) > 0
    own_cols = jnp.where(kept_tiles, own_tiles, jnp.zeros((), own_tiles.dtype)).reshape(
        -1, tile_rows, col_width
    )
    pair_cols = pair_blocks.reshape(-1, tile_rows, col_width)
    root_cols = root_blocks.reshape(-1, tile_rows, col_width)
    own_inv = own_inverse.reshape(-1, tile_rows, col_width)
    pair_inv = pair_inverse.reshape(-1, tile_rows, col_width)
    root_inv = root_inverse.reshape(-1, tile_rows, col_width)
    own_rows = own_rhs.reshape(-1, tile_rows, rhs_width)
    shared_rows = shared_rhs.reshape(-1, tile_rows, rhs_width)
    panels = own_inv.shape[0]
    solved = jnp.stack(
        forward_solve(
            own_cols, own_inv, pair_cols, pair_inv, root_cols, root_inv, own_rows, shared_rows
        )
    )
    solved = solved.reshape(3 * panels, cycles, 1, tile_rows, rhs_width)
    return (solved[:panels][None], solved[panels : 2 * panels][None], solved[2 * panels :][None])


def solution(mesh):
    return jax.shard_map(
        local,
        mesh=mesh,
        in_specs=(
            P("layer", None, "prow", None, None, "pcol", None),
            P("layer", None, "prow", None, "pcol"),
            P("layer", None, "prow", None, None, "pcol", None),
            P("layer", None, "prow", None, None, "pcol", None),
            P("layer", None, "prow", None, None, "pcol", None),
            P(None, "prow", None, None, "pcol", None),
            P(None, "prow", None, None, "pcol", None),
            P("layer", None, "prow", None, None),
            P("layer", None, "prow", None, None),
        ),
        out_specs=(
            P("layer", None, None, "pcol", None, None),
            P("layer", None, None, "pcol", None, None),
            P("layer", None, None, "pcol", None, None),
        ),
        check_vma=False,
    )
```

profile of v0, /device:TPU:2, one launch (start us, length us, event | category | flops | bytes accessed | tf_op | source)
XLA Modules:
  0.0 1858.6 jit_solution(14308534549543791466)
XLA Ops:
  8.3 1.7 convolution_convert_fusion.8
  10.8 2.5 broadcast_select_fusion
  14.1 135.7 %all-reduce.18.cloned.1.call-done = bf16[256,256]{1,0:T(8,128)(2,1)} async-done(((bf16[256,256]{1,0:T(8,128)(2,1)}), bf16[256,256]{1,0:T(8,128)(2,1)}) %all-reduce.18.cloned.1.call-update) | async-done | bytes 131088 | tf_op jit(solution)/shard_map/psum | solution.py:27
  151.7 70.0 %all-reduce.20.cloned.1.call-done = bf16[128,256]{1,0:T(8,128)(2,1)} async-done(((bf16[128,256]{1,0:T(8,128)(2,1)}), bf16[128,256]{1,0:T(8,128)(2,1)}) %all-reduce.20.cloned.1.call-update) | async-done | bytes 65552 | tf_op jit(solution)/shard_map/psum | solution.py:19
  221.8 1.7 fusion.3
  225.0 135.4 %all-reduce.22.cloned.1.call-done = bf16[256,256]{0,1:T(8,128)(2,1)} async-done(((bf16[256,256]{0,1:T(8,128)(2,1)}), bf16[256,256]{0,1:T(8,128)(2,1)}) %all-reduce.22.cloned.1.call-update) | async-done | bytes 131088 | tf_op jit(solution)/shard_map/psum | solution.py:27
  362.5 69.7 %all-reduce.24.cloned.1.call-done = bf16[128,256]{1,0:T(8,128)(2,1)} async-done(((bf16[128,256]{1,0:T(8,128)(2,1)}), bf16[128,256]{1,0:T(8,128)(2,1)}) %all-reduce.24.cloned.1.call-update) | async-done | bytes 65552 | tf_op jit(solution)/shard_map/psum | solution.py:19
  432.2 1.7 fusion.4
  434.5 136.1 %all-reduce.26.cloned.1.call-done = bf16[256,256]{0,1:T(8,128)(2,1)} async-done(((bf16[256,256]{0,1:T(8,128)(2,1)}), bf16[256,256]{0,1:T(8,128)(2,1)}) %all-reduce.26.cloned.1.call-update) | async-done | bytes 131088 | tf_op jit(solution)/shard_map/psum | solution.py:27
  571.9 3.5 collective-permute-start
  575.4 6.3 collective-permute-done
  582.6 68.9 %all-reduce.28.cloned.1.call-done = bf16[128,256]{1,0:T(8,128)(2,1)} async-done(((bf16[128,256]{1,0:T(8,128)(2,1)}), bf16[128,256]{1,0:T(8,128)(2,1)}) %all-reduce.28.cloned.1.call-update) | async-done | bytes 65552 | tf_op jit(solution)/shard_map/psum | solution.py:19
  651.5 1.7 fusion.5
  653.3 136.8 %all-reduce.30.cloned.1.call-done = bf16[256,256]{0,1:T(8,128)(2,1)} async-done(((bf16[256,256]{0,1:T(8,128)(2,1)}), bf16[256,256]{0,1:T(8,128)(2,1)}) %all-reduce.30.cloned.1.call-update) | async-done | bytes 131088 | tf_op jit(solution)/shard_map/psum | solution.py:27
  792.0 70.0 %all-reduce.32.cloned.1.call-done = bf16[128,256]{1,0:T(8,128)(2,1)} async-done(((bf16[128,256]{1,0:T(8,128)(2,1)}), bf16[128,256]{1,0:T(8,128)(2,1)}) %all-reduce.32.cloned.1.call-update) | async-done | bytes 65552 | tf_op jit(solution)/shard_map/psum | solution.py:19
  862.0 1.7 fusion.6
  863.8 136.8 %all-reduce.34.cloned.1.call-done = bf16[256,256]{0,1:T(8,128)(2,1)} async-done(((bf16[256,256]{0,1:T(8,128)(2,1)}), bf16[256,256]{0,1:T(8,128)(2,1)}) %all-reduce.34.cloned.1.call-update) | async-done | bytes 131088 | tf_op jit(solution)/shard_map/psum | solution.py:27
  1002.5 69.9 %all-reduce.36.cloned.1.call-done = bf16[128,256]{1,0:T(8,128)(2,1)} async-done(((bf16[128,256]{1,0:T(8,128)(2,1)}), bf16[128,256]{1,0:T(8,128)(2,1)}) %all-reduce.36.cloned.1.call-update) | async-done | bytes 65552 | tf_op jit(solution)/shard_map/psum | solution.py:19
  1072.4 1.7 fusion.7
  1074.2 136.8 %all-reduce.38.cloned.1.call-done = bf16[256,256]{0,1:T(8,128)(2,1)} async-done(((bf16[256,256]{0,1:T(8,128)(2,1)}), bf16[256,256]{0,1:T(8,128)(2,1)}) %all-reduce.38.cloned.1.call-update) | async-done | bytes 131088 | tf_op jit(solution)/shard_map/psum | solution.py:27
  1212.3 5.0 collective-permute-start.1
  1217.3 4.1 collective-permute-done.1
  1222.5 68.8 %all-reduce.40.cloned.1.call-done = bf16[128,256]{1,0:T(8,128)(2,1)} async-done(((bf16[128,256]{1,0:T(8,128)(2,1)}), bf16[128,256]{1,0:T(8,128)(2,1)}) %all-reduce.40.cloned.1.call-update) | async-done | bytes 65552 | tf_op jit(solution)/shard_map/psum | solution.py:19
  1291.3 1.7 fusion.8
  1293.1 136.8 %all-reduce.42.cloned.1.call-done = bf16[256,256]{0,1:T(8,128)(2,1)} async-done(((bf16[256,256]{0,1:T(8,128)(2,1)}), bf16[256,256]{0,1:T(8,128)(2,1)}) %all-reduce.42.cloned.1.call-update) | async-done | bytes 131088 | tf_op jit(solution)/shard_map/psum | solution.py:27
  1431.8 69.9 %all-reduce.44.cloned.1.call-done = bf16[128,256]{1,0:T(8,128)(2,1)} async-done(((bf16[128,256]{1,0:T(8,128)(2,1)}), bf16[128,256]{1,0:T(8,128)(2,1)}) %all-reduce.44.cloned.1.call-update) | async-done | bytes 65552 | tf_op jit(solution)/shard_map/psum | solution.py:19
  1501.7 1.7 fusion.9
  1503.5 136.6 %all-reduce.46.cloned.1.call-done = bf16[256,256]{0,1:T(8,128)(2,1)} async-done(((bf16[256,256]{0,1:T(8,128)(2,1)}), bf16[256,256]{0,1:T(8,128)(2,1)}) %all-reduce.46.cloned.1.call-update) | async-done | bytes 131088 | tf_op jit(solution)/shard_map/psum | solution.py:27
  1640.2 1.8 fusion.21
  1642.2 69.7 %all-reduce.48.cloned.1.call-done = bf16[128,256]{1,0:T(8,128)(2,1)} async-done(((bf16[128,256]{1,0:T(8,128)(2,1)}), bf16[128,256]{1,0:T(8,128)(2,1)}) %all-reduce.48.cloned.1.call-update) | async-done | bytes 65552 | tf_op jit(solution)/shard_map/psum | solution.py:19
  1711.9 1.8 convolution_convert_fusion
  1715.9 134.5 %all-reduce.50.cloned.1.call-done = bf16[1,1,2,1,128,256]{5,4,3,2,1,0:T(8,128)(2,1)} async-done(((bf16[1,1,2,1,128,256]{5,4,3,2,1,0:T(8,128)(2,1)}), bf16[1,1,2,1,128,256]{5,4,3,2,1,0:T(8,128)(2,1)}) %all-reduce.50.cloned.1.call-update) | async-done | bytes 131088 | tf_op jit(solution)/shard_map/psum | solution.py:27
  (104 shorter events, 22.9 us)
Async XLA Ops:
  7.2 142.7 %all-reduce.18.cloned.1.call-start = ((), (), s32[]{:S(2)}) async-start(), calls=%async_computation | async-start | bytes 262144 | tf_op jit(solution)/shard_map/psum | solution.py:27
  10.0 211.8 %all-reduce.20.cloned.1.call-start = ((), (), s32[]{:S(2)}) async-start(), calls=%async_computation.1 | async-start | bytes 131072 | tf_op jit(solution)/shard_map/psum | solution.py:19
  151.7 208.7 %all-reduce.22.cloned.1.call-start = ((), (), s32[]{:S(2)}) async-start(), calls=%async_computation.2 | async-start | bytes 262144 | tf_op jit(solution)/shard_map/psum | solution.py:27
  223.5 208.6 %all-reduce.24.cloned.1.call-start = ((), (), s32[]{:S(2)}) async-start(), calls=%async_computation.3 | async-start | bytes 131072 | tf_op jit(solution)/shard_map/psum | solution.py:19
  361.7 208.9 %copy-start.8 = (bf16[1,6,1,128,256]{4,3,2,1,0:T(8,128)(2,1)S(1)}, bf16[1,6,1,128,256]{4,3,2,1,0:T(8,128)(2,1)}, u32[]{:S(2)}) copy-start(bf16[1,6,1,128,256]{4,3,2,1,0:T(8,128)(2,1)} %param.33) | copy-start | bytes 1179652
  362.4 208.2 %all-reduce.26.cloned.1.call-start = ((), (), s32[]{:S(2)}) async-start(), calls=%async_computation.4 | async-start | bytes 262144 | tf_op jit(solution)/shard_map/psum | solution.py:27
  433.9 217.5 %all-reduce.28.cloned.1.call-start = ((), (), s32[]{:S(2)}) async-start(), calls=%async_computation.5 | async-start | bytes 131072 | tf_op jit(solution)/shard_map/psum | solution.py:19
  571.8 10.6 copy-start.9
  571.9 9.8 collective-permute-start
  581.7 208.4 %slice-start = ((bf16[1,12,1,128,2,1,128]{6,4,5,3,2,1,0:T(2,128)(2,1)}), bf16[1,5,1,128,2,1,128]{6,4,5,3,2,1,0:T(2,128)(2,1)S(1)}, s32[]{:S(2)}) async-start(bf16[1,12,1,128,2,1,128]{6,4,5,3,2,1,0:T(2,128)(2,1)} %param.28), calls=%async_computation.17 | async-start | bytes 655360 | tf_op jit(solution)/shard_map/slice | solution.py:61
  582.4 207.7 %all-reduce.30.cloned.1.call-start = ((), (), s32[]{:S(2)}) async-start(), calls=%async_computation.6 | async-start | bytes 262144 | tf_op jit(solution)/shard_map/psum | solution.py:27
  653.2 208.8 %all-reduce.32.cloned.1.call-start = ((), (), s32[]{:S(2)}) async-start(), calls=%async_computation.7 | async-start | bytes 131072 | tf_op jit(solution)/shard_map/psum | solution.py:19
  653.2 347.4 %slice-start.1 = ((bf16[1,12,1,128,2,1,128]{6,4,5,3,2,1,0:T(2,128)(2,1)}), bf16[1,4,1,128,2,1,128]{6,4,5,3,2,1,0:T(2,128)(2,1)S(1)}, s32[]{:S(2)}) async-start(bf16[1,12,1,128,2,1,128]{6,4,5,3,2,1,0:T(2,128)(2,1)} %param.28), calls=%async_computation.18 | async-start | bytes 524288 | tf_op jit(solution)/shard_map/slice | solution.py:61
  791.9 208.7 %all-reduce.34.cloned.1.call-start = ((), (), s32[]{:S(2)}) async-start(), calls=%async_computation.8 | async-start | bytes 262144 | tf_op jit(solution)/shard_map/psum | solution.py:27
  863.7 208.7 %all-reduce.36.cloned.1.call-start = ((), (), s32[]{:S(2)}) async-start(), calls=%async_computation.9 | async-start | bytes 131072 | tf_op jit(solution)/shard_map/psum | solution.py:19
  863.8 347.2 %slice-start.2 = ((bf16[1,12,1,128,2,1,128]{6,4,5,3,2,1,0:T(2,128)(2,1)}), bf16[1,3,1,128,2,1,128]{6,4,5,3,2,1,0:T(2,128)(2,1)S(1)}, s32[]{:S(2)}) async-start(bf16[1,12,1,128,2,1,128]{6,4,5,3,2,1,0:T(2,128)(2,1)} %param.28), calls=%async_computation.19 | async-start | bytes 393216 | tf_op jit(solution)/shard_map/slice | solution.py:61
  1002.5 208.6 %all-reduce.38.cloned.1.call-start = ((), (), s32[]{:S(2)}) async-start(), calls=%async_computation.10 | async-start | bytes 262144 | tf_op jit(solution)/shard_map/psum | solution.py:27
  1074.1 217.2 %all-reduce.40.cloned.1.call-start = ((), (), s32[]{:S(2)}) async-start(), calls=%async_computation.11 | async-start | bytes 131072 | tf_op jit(solution)/shard_map/psum | solution.py:19
  1212.3 217.6 %slice-start.3 = ((bf16[3,1,128,2,1,128]{5,3,4,2,1,0:T(2,128)(2,1)}), bf16[2,1,128,2,1,128]{5,3,4,2,1,0:T(2,128)(2,1)S(1)}, s32[]{:S(2)}) async-start(bf16[3,1,128,2,1,128]{5,3,4,2,1,0:T(2,128)(2,1)} %param.30), calls=%async_computation.20 | async-start | bytes 262144 | tf_op jit(solution)/shard_map/slice | solution.py:74
  1212.3 9.2 collective-permute-start.1
  1221.6 418.6 %slice-start.4 = ((bf16[3,1,128,2,1,128]{5,3,4,2,1,0:T(2,128)(2,1)}), bf16[1,1,128,2,1,128]{5,3,4,2,1,0:T(2,128)(2,1)S(1)}, s32[]{:S(2)}) async-start(bf16[3,1,128,2,1,128]{5,3,4,2,1,0:T(2,128)(2,1)} %param.30), calls=%async_computation.21 | async-start | bytes 131072 | tf_op jit(solution)/shard_map/slice | solution.py:74
  1222.2 207.7 %all-reduce.42.cloned.1.call-start = ((), (), s32[]{:S(2)}) async-start(), calls=%async_computation.12 | async-start | bytes 262144 | tf_op jit(solution)/shard_map/psum | solution.py:27
  1222.4 419.6 %copy-start = (bf16[256,256]{0,1:T(8,128)(2,1)S(1)}, bf16[256,256]{0,1:T(8,128)(2,1)}, u32[]{:S(2)}) copy-start(bf16[256,256]{0,1:T(8,128)(2,1)} %all-reduce.22.cloned.1.call-done) | copy-start | bytes 393220
  1293.0 349.1 %copy-start.1 = (bf16[256,256]{0,1:T(8,128)(2,1)S(1)}, bf16[256,256]{0,1:T(8,128)(2,1)}, u32[]{:S(2)}) copy-start(bf16[256,256]{0,1:T(8,128)(2,1)} %all-reduce.26.cloned.1.call-done) | copy-start | bytes 393220
  1293.0 208.7 %all-reduce.44.cloned.1.call-start = ((), (), s32[]{:S(2)}) async-start(), calls=%async_computation.13 | async-start | bytes 131072 | tf_op jit(solution)/shard_map/psum | solution.py:19
  1429.9 283.8 %copy-start.7 = (bf16[256,256]{1,0:T(8,128)(2,1)S(1)}, bf16[256,256]{1,0:T(8,128)(2,1)}, u32[]{:S(2)}) copy-start(bf16[256,256]{1,0:T(8,128)(2,1)} %all-reduce.18.cloned.1.call-done) | copy-start | bytes 393220
  1431.7 208.4 %all-reduce.46.cloned.1.call-start = ((), (), s32[]{:S(2)}) async-start(), calls=%async_computation.14 | async-start | bytes 262144 | tf_op jit(solution)/shard_map/psum | solution.py:27
  1501.7 212.8 %copy-start.2 = (bf16[256,256]{0,1:T(8,128)(2,1)S(1)}, bf16[256,256]{0,1:T(8,128)(2,1)}, u32[]{:S(2)}) copy-start(bf16[256,256]{0,1:T(8,128)(2,1)} %all-reduce.30.cloned.1.call-done) | copy-start | bytes 393220
  1503.5 211.2 %copy-start.6 = (bf16[256,256]{0,1:T(8,128)(2,1)S(1)}, bf16[256,256]{0,1:T(8,128)(2,1)}, u32[]{:S(2)}) copy-start(bf16[256,256]{0,1:T(8,128)(2,1)} %all-reduce.34.cloned.1.call-done) | copy-start | bytes 393220
  1503.5 208.5 %all-reduce.48.cloned.1.call-start = ((), (), s32[]{:S(2)}) async-start(), calls=%async_computation.15 | async-start | bytes 131072 | tf_op jit(solution)/shard_map/psum | solution.py:19
  1640.2 74.6 %copy-start.3 = (bf16[256,256]{0,1:T(8,128)(2,1)S(1)}, bf16[256,256]{0,1:T(8,128)(2,1)}, u32[]{:S(2)}) copy-start(bf16[256,256]{0,1:T(8,128)(2,1)} %all-reduce.38.cloned.1.call-done) | copy-start | bytes 393220
  1642.0 208.4 %all-reduce.50.cloned.1.call-start = ((), (), s32[]{:S(2)}) async-start(), calls=%async_computation.16 | async-start | bytes 262144 | tf_op jit(solution)/shard_map/psum | solution.py:27
  (3 other events, 15.9 us)
Sparse Core Ops, SparseCore 0:
  10.9 138.9 all-reduce.17
  152.8 68.9 all-reduce.19
  224.6 135.6 all-reduce.21
  363.2 68.9 all-reduce.23
  434.9 135.6 all-reduce.25
  582.5 68.8 all-reduce.27
  654.3 135.6 all-reduce.29
  793.1 68.9 all-reduce.31
  864.9 135.6 all-reduce.33
  1003.5 68.9 all-reduce.35
  1075.3 135.6 all-reduce.37
  1222.4 68.8 all-reduce.39
  1294.2 135.6 all-reduce.41
  1432.7 68.9 all-reduce.43
  1504.4 135.6 all-reduce.45
  1643.0 68.9 all-reduce.47
  1714.7 135.6 all-reduce.49
where the time goes:
time: 1860 us
  waiting for transfers between devices  1790 us (96%)
  matrix products  25.7 us (1%)
    psum x9, waiting for transfers between devices, panel_solve(): return lax.psum(partial_value.astype(jnp.bfloat16), 'prow')  1230 us
    psum x8, waiting for transfers between devices, row_total(): lax.psum(partial_value.astype(jnp.bfloat16), 'pcol').astype(jnp.float32)  557 us
  transfers between devices with their start and end apart: 19, of which 19 were waited for; matrix products, arithmetic and copies ran while one was open for 0% of the time, Pallas kernels for 0%

commit v1 on v0

--- a/solution.py
+++ b/solution.py
@@ -16,7 +16,9 @@
 
 
 def row_total(partial_value):
-    return lax.psum(partial_value.astype(jnp.bfloat16), "pcol").astype(jnp.float32)
+    return jnp.sum(lax.all_gather(partial_value.astype(jnp.bfloat16), "pcol"), axis=0).astype(
+        jnp.float32
+    )
 
 
 def panel_solve(residual, inverse):

time: 1860 us -> 1350 us (0.73)
  waiting for transfers between devices: 1790 us -> 1190 us
  blocking collectives: 0 us -> 105 us
    psum x8 -> x0, waiting for transfers between devices: 557 us -> none  [row_total(): lax.psum(partial_value.astype(jnp.bfloat16), 'pcol').astype(jnp.float32)]
    all_gather x0 -> x8, blocking collectives: none -> 105 us  [row_total(): lax.all_gather(partial_value.astype(jnp.bfloat16), 'pcol')]
    psum x9, waiting for transfers between devices: 1230 us -> 1180 us  [panel_solve(): return lax.psum(partial_value.astype(jnp.bfloat16), 'prow')]
  transfers between devices with their start and end apart: 19 -> 11, of which waited for: 19 -> 11; matrix products, arithmetic and copies ran while one was open for 0% -> 1% of each run, Pallas kernels for 0% -> 0%
where the time goes in v1:
time: 1350 us
  waiting for transfers between devices  1190 us (88%)
  blocking collectives  105 us (8%)
  matrix products  19.9 us (1%)
  between operations  14.3 us (1%)
    psum x9, waiting for transfers between devices, panel_solve(): return lax.psum(partial_value.astype(jnp.bfloat16), 'prow')  1180 us
    all_gather x8, blocking collectives, row_total(): lax.all_gather(partial_value.astype(jnp.bfloat16), 'pcol')  105 us
  transfers between devices with their start and end apart: 11, of which 11 were waited for; matrix products, arithmetic and copies ran while one was open for 1% of the time, Pallas kernels for 0%

profile of v1, /device:TPU:2, one launch (start us, length us, event | category | flops | bytes accessed | tf_op | source)
XLA Modules:
  0.0 1351.2 jit_solution(7608456566844619697)
XLA Ops:
  8.3 1.7 convolution_convert_fusion.8
  10.8 2.5 broadcast_select_fusion
  14.1 135.7 %all-reduce.10.cloned.1.call-done = bf16[256,256]{1,0:T(8,128)(2,1)} async-done(((bf16[256,256]{1,0:T(8,128)(2,1)}), bf16[256,256]{1,0:T(8,128)(2,1)}) %all-reduce.10.cloned.1.call-update) | async-done | bytes 131088 | tf_op jit(solution)/shard_map/psum | solution.py:29
  149.8 1.2 fusion.34
  151.0 13.1 all_gather.32
  164.2 1.7 fusion.3
  167.4 129.7 %all-reduce.12.cloned.1.call-done = bf16[256,256]{0,1:T(8,128)(2,1)} async-done(((bf16[256,256]{0,1:T(8,128)(2,1)}), bf16[256,256]{0,1:T(8,128)(2,1)}) %all-reduce.12.cloned.1.call-update) | async-done | bytes 131088 | tf_op jit(solution)/shard_map/psum | solution.py:29
  297.2 1.3 convolution_add_fusion
  298.5 13.1 all_gather.33
  311.7 1.7 fusion.4
  314.1 130.6 %all-reduce.14.cloned.1.call-done = bf16[256,256]{0,1:T(8,128)(2,1)} async-done(((bf16[256,256]{0,1:T(8,128)(2,1)}), bf16[256,256]{0,1:T(8,128)(2,1)}) %all-reduce.14.cloned.1.call-update) | async-done | bytes 131088 | tf_op jit(solution)/shard_map/psum | solution.py:29
  444.7 1.2 fusion.71
  445.9 3.4 collective-permute-start
  449.4 6.1 collective-permute-done
  455.7 13.2 all_gather.34
  469.9 131.1 %all-reduce.16.cloned.1.call-done = bf16[256,256]{0,1:T(8,128)(2,1)} async-done(((bf16[256,256]{0,1:T(8,128)(2,1)}), bf16[256,256]{0,1:T(8,128)(2,1)}) %all-reduce.16.cloned.1.call-update) | async-done | bytes 131088 | tf_op jit(solution)/shard_map/psum | solution.py:29
  601.1 1.2 convolution_bitcast_fusion
  602.3 13.2 all_gather.35
  616.6 131.1 %all-reduce.18.cloned.1.call-done = bf16[256,256]{0,1:T(8,128)(2,1)} async-done(((bf16[256,256]{0,1:T(8,128)(2,1)}), bf16[256,256]{0,1:T(8,128)(2,1)}) %all-reduce.18.cloned.1.call-update) | async-done | bytes 131088 | tf_op jit(solution)/shard_map/psum | solution.py:29
  747.7 1.2 fusion.1
  748.9 13.3 all_gather.36
  763.1 131.1 %all-reduce.20.cloned.1.call-done = bf16[256,256]{0,1:T(8,128)(2,1)} async-done(((bf16[256,256]{0,1:T(8,128)(2,1)}), bf16[256,256]{0,1:T(8,128)(2,1)}) %all-reduce.20.cloned.1.call-update) | async-done | bytes 131088 | tf_op jit(solution)/shard_map/psum | solution.py:29
  895.5 4.9 collective-permute-start.1
  900.6 4.0 collective-permute-done.1
  904.7 13.1 all_gather.37
  918.8 131.1 %all-reduce.22.cloned.1.call-done = bf16[256,256]{0,1:T(8,128)(2,1)} async-done(((bf16[256,256]{0,1:T(8,128)(2,1)}), bf16[256,256]{0,1:T(8,128)(2,1)}) %all-reduce.22.cloned.1.call-update) | async-done | bytes 131088 | tf_op jit(solution)/shard_map/psum | solution.py:29
  1049.9 1.2 convolution_bitcast_fusion.3
  1051.1 13.1 all_gather.38
  1065.5 130.9 %all-reduce.24.cloned.1.call-done = bf16[256,256]{0,1:T(8,128)(2,1)} async-done(((bf16[256,256]{0,1:T(8,128)(2,1)}), bf16[256,256]{0,1:T(8,128)(2,1)}) %all-reduce.24.cloned.1.call-update) | async-done | bytes 131088 | tf_op jit(solution)/shard_map/psum | solution.py:29
  1197.5 13.3 all_gather.39
  1214.0 129.0 %all-reduce.26.cloned.1.call-done = bf16[1,1,2,1,128,256]{5,4,3,2,1,0:T(8,128)(2,1)} async-done(((bf16[1,1,2,1,128,256]{5,4,3,2,1,0:T(8,128)(2,1)}), bf16[1,1,2,1,128,256]{5,4,3,2,1,0:T(8,128)(2,1)}) %all-reduce.26.cloned.1.call-update) | async-done | bytes 131088 | tf_op jit(solution)/shard_map/psum | solution.py:29
  1343.0 1.7 pad_maximum_fusion.2
  (96 shorter events, 16.0 us)
Async XLA Ops:
  7.2 142.7 %all-reduce.10.cloned.1.call-start = ((), (), s32[]{:S(2)}) async-start(), calls=%async_computation | async-start | bytes 262144 | tf_op jit(solution)/shard_map/psum | solution.py:29
  10.0 287.2 %all-reduce.12.cloned.1.call-start = ((), (), s32[]{:S(2)}) async-start(), calls=%async_computation.1 | async-start | bytes 262144 | tf_op jit(solution)/shard_map/psum | solution.py:29
  166.0 278.7 %all-reduce.14.cloned.1.call-start = ((), (), s32[]{:S(2)}) async-start(), calls=%async_computation.2 | async-start | bytes 262144 | tf_op jit(solution)/shard_map/psum | solution.py:29
  311.6 133.0 %copy-start.8 = (bf16[1,6,1,128,256]{4,3,2,1,0:T(8,128)(2,1)S(1)}, bf16[1,6,1,128,256]{4,3,2,1,0:T(8,128)(2,1)}, u32[]{:S(2)}) copy-start(bf16[1,6,1,128,256]{4,3,2,1,0:T(8,128)(2,1)} %param.33) | copy-start | bytes 1179652
  313.5 287.6 %all-reduce.16.cloned.1.call-start = ((), (), s32[]{:S(2)}) async-start(), calls=%async_computation.3 | async-start | bytes 262144 | tf_op jit(solution)/shard_map/psum | solution.py:29
  314.1 135.2 %copy-start.9 = (bf16[1,3,1,128,2,1,128]{6,4,5,3,2,1,0:T(2,128)(2,1)S(1)}, bf16[1,3,1,128,2,1,128]{6,4,5,3,2,1,0:T(2,128)(2,1)}, u32[]{:S(2)}) copy-start(bf16[1,3,1,128,2,1,128]{6,4,5,3,2,1,0:T(2,128)(2,1)} %param.29) | copy-start | bytes 589828
  445.9 9.7 collective-permute-start
  455.6 145.4 %slice-start = ((bf16[1,12,1,128,2,1,128]{6,4,5,3,2,1,0:T(2,128)(2,1)}), bf16[1,5,1,128,2,1,128]{6,4,5,3,2,1,0:T(2,128)(2,1)S(1)}, s32[]{:S(2)}) async-start(bf16[1,12,1,128,2,1,128]{6,4,5,3,2,1,0:T(2,128)(2,1)} %param.28), calls=%async_computation.9 | async-start | bytes 655360 | tf_op jit(solution)/shard_map/slice | solution.py:63
  469.9 277.8 %all-reduce.18.cloned.1.call-start = ((), (), s32[]{:S(2)}) async-start(), calls=%async_computation.4 | async-start | bytes 262144 | tf_op jit(solution)/shard_map/psum | solution.py:29
  602.2 145.4 %slice-start.1 = ((bf16[1,12,1,128,2,1,128]{6,4,5,3,2,1,0:T(2,128)(2,1)}), bf16[1,4,1,128,2,1,128]{6,4,5,3,2,1,0:T(2,128)(2,1)S(1)}, s32[]{:S(2)}) async-start(bf16[1,12,1,128,2,1,128]{6,4,5,3,2,1,0:T(2,128)(2,1)} %param.28), calls=%async_computation.10 | async-start | bytes 524288 | tf_op jit(solution)/shard_map/slice | solution.py:63
  616.5 277.8 %all-reduce.20.cloned.1.call-start = ((), (), s32[]{:S(2)}) async-start(), calls=%async_computation.5 | async-start | bytes 262144 | tf_op jit(solution)/shard_map/psum | solution.py:29
  748.8 145.4 %slice-start.2 = ((bf16[1,12,1,128,2,1,128]{6,4,5,3,2,1,0:T(2,128)(2,1)}), bf16[1,3,1,128,2,1,128]{6,4,5,3,2,1,0:T(2,128)(2,1)S(1)}, s32[]{:S(2)}) async-start(bf16[1,12,1,128,2,1,128]{6,4,5,3,2,1,0:T(2,128)(2,1)} %param.28), calls=%async_computation.11 | async-start | bytes 393216 | tf_op jit(solution)/shard_map/slice | solution.py:63
  763.1 137.4 %copy-start.10 = (bf16[3,1,128,2,1,128]{5,3,4,2,1,0:T(2,128)(2,1)S(1)}, bf16[3,1,128,2,1,128]{5,3,4,2,1,0:T(2,128)(2,1)}, u32[]{:S(2)}) copy-start(bf16[3,1,128,2,1,128]{5,3,4,2,1,0:T(2,128)(2,1)} %param.31) | copy-start | bytes 589828
  763.1 286.8 %all-reduce.22.cloned.1.call-start = ((), (), s32[]{:S(2)}) async-start(), calls=%async_computation.6 | async-start | bytes 262144 | tf_op jit(solution)/shard_map/psum | solution.py:29
  895.5 9.1 collective-permute-start.1
  900.6 149.3 %slice-start.3 = ((bf16[3,1,128,2,1,128]{5,3,4,2,1,0:T(2,128)(2,1)}), bf16[2,1,128,2,1,128]{5,3,4,2,1,0:T(2,128)(2,1)S(1)}, s32[]{:S(2)}) async-start(bf16[3,1,128,2,1,128]{5,3,4,2,1,0:T(2,128)(2,1)} %param.30), calls=%async_computation.12 | async-start | bytes 262144 | tf_op jit(solution)/shard_map/slice | solution.py:76
  918.7 146.5 %copy-start = (bf16[256,256]{0,1:T(8,128)(2,1)S(1)}, bf16[256,256]{0,1:T(8,128)(2,1)}, u32[]{:S(2)}) copy-start(bf16[256,256]{0,1:T(8,128)(2,1)} %all-reduce.12.cloned.1.call-done) | copy-start | bytes 393220
  918.8 277.6 %all-reduce.24.cloned.1.call-start = ((), (), s32[]{:S(2)}) async-start(), calls=%async_computation.7 | async-start | bytes 262144 | tf_op jit(solution)/shard_map/psum | solution.py:29
  1049.9 15.5 %copy-start.1 = (bf16[256,256]{0,1:T(8,128)(2,1)S(1)}, bf16[256,256]{0,1:T(8,128)(2,1)}, u32[]{:S(2)}) copy-start(bf16[256,256]{0,1:T(8,128)(2,1)} %all-reduce.14.cloned.1.call-done) | copy-start | bytes 393220
  1051.1 145.3 %slice-start.4 = ((bf16[3,1,128,2,1,128]{5,3,4,2,1,0:T(2,128)(2,1)}), bf16[1,1,128,2,1,128]{5,3,4,2,1,0:T(2,128)(2,1)S(1)}, s32[]{:S(2)}) async-start(bf16[3,1,128,2,1,128]{5,3,4,2,1,0:T(2,128)(2,1)} %param.30), calls=%async_computation.13 | async-start | bytes 131072 | tf_op jit(solution)/shard_map/slice | solution.py:76
  1065.2 146.6 %copy-start.7 = (bf16[256,256]{1,0:T(8,128)(2,1)S(1)}, bf16[256,256]{1,0:T(8,128)(2,1)}, u32[]{:S(2)}) copy-start(bf16[256,256]{1,0:T(8,128)(2,1)} %all-reduce.10.cloned.1.call-done) | copy-start | bytes 393220
  1065.2 277.7 %all-reduce.26.cloned.1.call-start = ((), (), s32[]{:S(2)}) async-start(), calls=%async_computation.8 | async-start | bytes 262144 | tf_op jit(solution)/shard_map/psum | solution.py:29
  1196.4 16.2 %copy-start.2 = (bf16[256,256]{0,1:T(8,128)(2,1)S(1)}, bf16[256,256]{0,1:T(8,128)(2,1)}, u32[]{:S(2)}) copy-start(bf16[256,256]{0,1:T(8,128)(2,1)} %all-reduce.16.cloned.1.call-done) | copy-start | bytes 393220
  1197.5 15.2 %copy-start.6 = (bf16[256,256]{0,1:T(8,128)(2,1)S(1)}, bf16[256,256]{0,1:T(8,128)(2,1)}, u32[]{:S(2)}) copy-start(bf16[256,256]{0,1:T(8,128)(2,1)} %all-reduce.18.cloned.1.call-done) | copy-start | bytes 393220
  1197.5 15.3 %copy-start.3 = (bf16[256,256]{0,1:T(8,128)(2,1)S(1)}, bf16[256,256]{0,1:T(8,128)(2,1)}, u32[]{:S(2)}) copy-start(bf16[256,256]{0,1:T(8,128)(2,1)} %all-reduce.20.cloned.1.call-done) | copy-start | bytes 393220
  1210.9 2.9 copy-start.4
  1211.8 2.1 copy-start.5
Sparse Core Ops, SparseCore 0:
  10.9 138.9 all-reduce.9
  166.1 131.0 all-reduce.11
  313.6 131.0 all-reduce.13
  470.0 131.0 all-reduce.15
  616.6 130.9 all-reduce.17
  763.2 131.0 all-reduce.19
  918.9 130.9 all-reduce.21
  1065.3 131.0 all-reduce.23
  1211.9 130.9 all-reduce.25
